TPU v7x, 32 devices: a whole 2x2x4 slice. The times are simulated.
32 devices in a mesh: rows: 8 (over z, x), modes: 4 (over y, core).
Axes of the slice: x: 2, y: 2, z: 4, core: 2. Of those that a mesh axis runs over, the one named last changes fastest.
Arguments:
- snapshots: bfloat16 [1024, 5, 6144], P(None, None, 'rows')
- eigvec: bfloat16 [1024, 256], P('rows', 'modes'), may hold values from -0.1875 to 0.1875
- eigval: float32 [256], replicated, may hold values from 30720 to 245760
- jac_self: bfloat16 [5, 5, 6144], P(None, None, 'rows'), may hold values from -0.5 to 1.5
- jac_off: bfloat16 [6, 5, 5, 6144], P(None, None, None, 'rows'), may hold values from -1 to 1
- neighbor: int32 [6, 6144], P(None, 'rows'), may hold values from 0 to 1279
- send_list: int32 [2, 2048], P(None, 'rows'), may hold values from 0 to 767
- send_count: int32 [2, 8], P(None, 'rows'), may hold values from 1 to 256
- owned_cells: int32 [8], P('rows'), may hold values from 1 to 768, 4608 in all
Outputs:
- test_basis: bfloat16 [256, 5, 6144], P('modes', None, 'rows')
- reduced: float32 [256, 256], P('rows', 'modes')
Inputs may be any that keep to these rules, and one draw needn't show every extreme that they name: neighbor[b, c] indexes the extended slots of the cell's own partition: its 768 own slots, then 256 lower ghost slots, then 256 upper ghost slots. `send_list`: entries of partition p's lists are local slots of partition p.
All inputs are finite; a program needn't handle non-finite values. No bound on the sum of `owned_cells` on one device may be relied on, other than what follows from the above.
Results may differ from a plain program's by a relative error of at most 0.0049.
Values may be sent and summed in bfloat16 or wider, within the bound.
A program may use at most 128 MiB of HBM per device.

v0:
```python
import jax
import jax.numpy as jnp
from jax import lax
from jax.sharding import PartitionSpec as P


def passed_along(value, axis, steps):
    count = lax.axis_size(axis)
    first, last = (max(0, -steps), min(count, count - steps))
    return lax.ppermute(value, axis, [(source, source + steps) for source in range(first, last)])


def neighbour_rows(piece, offset):
    return passed_along(piece, "rows", offset)


def shards(
    snapshots, eigvec, eigval, jac_self, jac_off, neighbor, send_list, send_count, owned_cells
):
    snap_count, var_count, cell_count = snapshots.shape
    panel_width = eigvec.shape[1]
    halo_slots = send_list.shape[1]
    snap_rows = snapshots.reshape(snap_count, var_count * cell_count)
    modes_sum = lax.dot_general(
        lax.all_gather(eigvec, "rows", axis=0, tiled=True),
        snap_rows,
        (((0,), (0,)), ((), ())),
        preferred_element_type=jnp.float32,
    )
    owned_mask = jnp.arange(cell_count, dtype=jnp.int32)[None, None, :] < owned_cells[0]
    modes = jnp.where(
        owned_mask,
        modes_sum.reshape(panel_width, var_count, cell_count),
        jnp.zeros((), jnp.float32),
    ).astype(jnp.bfloat16)
    picked = jnp.take(modes, send_list.reshape(-1), axis=2).reshape(
        panel_width, var_count, 2, halo_slots
    )
    live_slots = jnp.arange(halo_slots, dtype=jnp.int32)[None, :] < send_count
    picked = jnp.where(live_slots[None, None], picked, jnp.zeros((), jnp.bfloat16))
    from_below = neighbour_rows(picked[:, :, 1], 1)
    from_above = neighbour_rows(picked[:, :, 0], -1)
    extended = jnp.concatenate([modes, from_below, from_above], axis=2)
    own_term = jnp.einsum("vwc,mwc->mvc", jac_self, modes, preferred_element_type=jnp.float32)
    neighbours = jnp.take(extended, neighbor, axis=2)
    off_term = jnp.einsum("bvwc,mwbc->mvc", jac_off, neighbours, preferred_element_type=jnp.float32)
    test_local = jnp.where(owned_mask, own_term + off_term, jnp.zeros((), jnp.float32)).astype(
        jnp.bfloat16
    )
    products = lax.dot_general(
        snap_rows,
        test_local.reshape(panel_width, var_count * cell_count),
        (((1,), (1,)), ((), ())),
        preferred_element_type=jnp.float32,
    )
    shares = lax.psum_scatter(products, "rows", scatter_dimension=0, tiled=True)
    eigvec_rows = lax.all_gather(eigvec, "modes", axis=1, tiled=True)
    partial_sum = jnp.dot(
        eigvec_rows.astype(jnp.float32).T, shares, precision=lax.Precision.HIGHEST
    )
    reduced_part = lax.psum_scatter(partial_sum, "rows", scatter_dimension=0, tiled=True)
    rows_out = reduced_part.shape[0]
    scales = 1.0 / jnp.sqrt(eigval)
    row_scales = lax.dynamic_slice_in_dim(scales, lax.axis_index("rows") * rows_out, rows_out, 0)
    col_scales = lax.dynamic_slice_in_dim(
        scales, lax.axis_index("modes") * panel_width, panel_width, 0
    )
    reduced = reduced_part * row_scales[:, None] * col_scales[None, :]
    return (test_local, reduced)


def solution(mesh):
    in_specs = (
        P(None, None, "rows"),
        P("rows", "modes"),
        P(),
        P(None, None, "rows"),
        P(None, None, None, "rows"),
        P(None, "rows"),
        P(None, "rows"),
        P(None, "rows"),
        P("rows"),
    )
    out_specs = (P("modes", None, "rows"), P("rows", "modes"))
    return jax.shard_map(shards, mesh=mesh, in_specs=in_specs, out_specs=out_specs, check_vma=False)
```

profile of v0, /device:TPU:0, one launch (start us, length us, event | category | flops | bytes accessed | tf_op | source)
XLA Modules:
  0.0 272.5 jit_solution(6265888050190093898)
XLA Ops:
  7.9 10.7 %copy.30 = bf16[1024,5,768]{0,2,1:T(8,128)(2,1)} copy(bf16[1024,5,768]{2,0,1:T(8,128)(2,1)} %param.9) | data formatting | bytes 15728640 | tf_op args[0]
  18.6 27.9 %all_gather.6 = bf16[1024,64]{0,1:T(8,128)(2,1)S(1)} all-gather(bf16[128,64]{0,1:T(8,128)(2,1)S(1)} %copy-done.3), channel_id=1, replica_groups=mesh['rows'=8,'modes'=4] {'rows'}, dimensions={0}, use_global_device_ids=true | all-gather | bytes 147456 | tf_op jit(solution)/shard_map/all_gather | solution.py:25
  46.5 5.7 %fusion.8 = bf16[64,5,768]{2,0,1:T(8,128)(2,1)S(1)} fusion(bf16[1024,5,768]{0,2,1:T(8,128)(2,1)} %copy.30, pred[768]{0:T(1024)(128)(4,1)S(1)} %iota_compare_fusion, bf16[1024,64]{0,1:T(8,128)(2,1)S(1)} %all_gather.6), kind=kOutput, calls=%fused_computation.10 | convolution fusion | flops 503808000 | bytes 8487680 | tf_op jit(solution)/shard_map/dot_general | solution.py:24
  52.2 1.1 copy.31
  53.4 1.8 gather_fusion
  55.2 0.5 copy.35
  55.7 0.1 compare_and_fusion.1
  55.8 3.4 %collective-permute-start = (bf16[64,5,256]{2,0,1:T(8,128)(2,1)S(1)}, bf16[64,5,256]{2,0,1:T(8,128)(2,1)S(1)}, u32[]{:S(2)}, u32[]{:S(2)}) collective-permute-start(bf16[64,5,256]{2,0,1:T(8,128)(2,1)S(1)} %get-tuple-element.8), channel_id=1, source_target_pairs={{0,4},{4,8},{8,12},{12,16},{16,20},{20,24},{24,28},{1,5},{5,9},{9,... | collective-permute-start | bytes 491528 | tf_op jit(solution)/shard_map/ppermute | solution.py:10
  59.2 1.5 collective-permute-start.1
  60.8 6.7 %copy.39 = bf16[6,5,5,768]{0,1,2,3:T(8,128)(2,1)} copy(bf16[6,5,5,768]{3,0,2,1:T(8,128)(2,1)} %param.13) | data formatting | bytes 460800 | tf_op args[4]
  67.5 1.9 copy.32
  69.4 1.0 pad_maximum_fusion
  70.4 2.9 %copy.36 = bf16[64,5,1280]{0,1,2:T(8,128)(2,1)S(1)} copy(bf16[64,5,1280]{2,0,1:T(8,128)(2,1)S(1)} %pad_maximum_fusion) | data formatting | bytes 1638400 | tf_op jit(solution)/shard_map/concatenate | solution.py:43
  73.3 12.9 %gather_fusion.1 = bf16[4608,64,5]{1,2,0:T(8,128)(2,1)} fusion(bf16[64,5,1280]{0,1,2:T(8,128)(2,1)S(1)} %copy.36, s32[5120]{0:T(1024)S(1)} %pad_clamp_fusion), kind=kCustom, calls=%fused_computation.1 | custom fusion | bytes 5916672 | tf_op jit(solution)/shard_map/jit(_take)/gather | solution.py:45
  86.2 9.9 %copy.46 = bf16[6,768,64,5]{1,0,2,3:T(8,128)(2,1)} copy(bf16[6,768,64,5]{2,3,1,0:T(8,128)(2,1)} %bitcast.58) | data formatting | bytes 5898240 | tf_op jit(solution)/shard_map/jit(_take)/gather | solution.py:45
  96.1 4.5 %select_bitcast_fusion = bf16[64,5,6,768]{3,2,0,1:T(8,128)(2,1)} fusion(bf16[6,768,64,5]{1,0,2,3:T(8,128)(2,1)} %copy.46, pred[6,768]{1,0:T(8,128)(4,1)S(1)} %compare_and_fusion), kind=kLoop, calls=%fused_computation.4 | loop fusion | flops 1474560 | bytes 5902848 | tf_op jit(solution)/shard_map/jit(_take)/select_n | solution.py:45
  100.5 14.5 %copy.38 = bf16[64,5,6,768]{0,2,1,3:T(8,128)(2,1)} copy(bf16[64,5,6,768]{3,2,0,1:T(8,128)(2,1)} %select_bitcast_fusion) | data formatting | bytes 5898240 | tf_op jit(solution)/shard_map/jit(_take)/select_n | solution.py:45
  115.0 9.6 %fusion.12 = f32[768,64,5,1]{1,2,3,0:T(8,128)S(1)} fusion(bf16[64,5,6,768]{0,2,1,3:T(8,128)(2,1)} %copy.38, bf16[6,5,5,768]{0,1,2,3:T(8,128)(2,1)} %copy.39), kind=kOutput, calls=%fused_computation.28 | convolution fusion | flops 14745600 | bytes 4162560 | tf_op jit(solution)/shard_map/bvwc,mwbc->mvc/dot_general | solution.py:46
  124.7 5.0 %fusion.4 = bf16[64,5,768]{0,1,2:T(8,128)(2,1)} fusion(f32[768,64,5,1]{1,2,3,0:T(8,128)S(1)} %fusion.12, bf16[64,5,768]{0,1,2:T(8,128)(2,1)} %copy-done, bf16[5,5,768]{1,0,2:T(8,128)(2,1)} %copy.32, pred[768]{0:T(1024)(128)(4,1)S(1)} %iota_compare_fusion), kind=kOutput, calls=%fused_computation.8 | convolution fusion | flops 3194880 | bytes 2005248 | tf_op jit(solution)/shard_map/vwc,mwc->mvc/dot_general | solution.py:44
  129.7 1.8 copy.41
  131.5 6.6 %convolution_bitcast_fusion = f32[1024,64]{0,1:T(8,128)} fusion(bf16[64,5,768]{2,0,1:T(8,128)(2,1)S(1)} %copy.41, bf16[1024,5,768]{2,0,1:T(8,128)(2,1)} %param.9), kind=kOutput, calls=%fused_computation.11 | convolution fusion | flops 503316480 | bytes 8617984 | tf_op jit(solution)/shard_map/dot_general | solution.py:50
  138.1 0.0 reduce-scatter.7.cloned.1.call-start
  138.2 5.2 %all_gather.7 = bf16[128,256]{0,1:T(8,128)(2,1)S(1)} all-gather(bf16[128,64]{0,1:T(8,128)(2,1)S(1)} %copy-done.3), channel_id=1, replica_groups=mesh['rows'=8,'modes'=4] {'modes'}, dimensions={1}, use_global_device_ids=true | all-gather | bytes 81920 | tf_op jit(solution)/shard_map/all_gather | solution.py:57
  143.4 57.5 %reduce-scatter.5.cloned.1.call-done = f32[128,64]{0,1:T(8,128)} async-done(((f32[1024,64]{0,1:T(8,128)}), f32[128,64]{0,1:T(8,128)}) %reduce-scatter.5.cloned.1.call-update) | async-done | bytes 32784 | tf_op jit(solution)/shard_map/reduce_scatter | solution.py:56
  200.9 1.0 convolution_bitcast_fusion.1
  201.9 0.8 copy.47
  202.7 0.1 dynamic_slice.6
  202.8 0.1 dynamic_slice.7
  202.8 61.3 %reduce-scatter.7.cloned.1.call-done = f32[32,64]{1,0:T(8,128)} async-done(((f32[256,64]{1,0:T(8,128)}), f32[32,64]{1,0:T(8,128)}) %reduce-scatter.7.cloned.1.call-update) | async-done | bytes 8208
  264.1 0.8 copy.48
  264.9 0.1 multiply_multiply_fusion
  265.0 0.7 copy.42
  (32 shorter events, 0.2 us)
Async XLA Ops:
  7.2 193.7 %reduce-scatter.5.cloned.1.call-start = ((), (), s32[]{:S(2)}) async-start(), calls=%async_computation.2 | async-start | bytes 294912 | tf_op jit(solution)/shard_map/reduce_scatter | solution.py:56
  7.9 10.7 %copy-start.3 = (bf16[128,64]{0,1:T(8,128)(2,1)S(1)}, bf16[128,64]{0,1:T(8,128)(2,1)}, u32[]{:S(2)}) copy-start(bf16[128,64]{0,1:T(8,128)(2,1)} %param.10) | copy-start | bytes 49156
  46.5 6.9 %copy-start.5 = (s32[2,256]{1,0:T(2,128)S(1)}, s32[2,256]{1,0:T(2,128)}, u32[]{:S(2)}) copy-start(s32[2,256]{1,0:T(2,128)} %param.15) | copy-start | bytes 6148
  52.2 3.5 %copy-start.7 = (s32[2,1]{0,1:T(1,128)S(1)}, s32[2,1]{0,1:T(1,128)}, u32[]{:S(2)}) copy-start(s32[2,1]{0,1:T(1,128)} %param.16) | copy-start | bytes 28
  52.2 8.5 %copy-start.2 = (s32[6,768]{1,0:T(8,128)S(1)}, s32[6,768]{1,0:T(8,128)}, u32[]{:S(2)}) copy-start(s32[6,768]{1,0:T(8,128)} %param.14) | copy-start | bytes 55300
  53.3 14.2 %copy-start = (bf16[64,5,768]{0,1,2:T(8,128)(2,1)}, bf16[64,5,768]{0,1,2:T(8,128)(2,1)S(1)}, u32[]{:S(2)}) copy-start(bf16[64,5,768]{0,1,2:T(8,128)(2,1)S(1)} %copy.31) | copy-start | bytes 1474564
  55.8 13.6 %collective-permute-start = (bf16[64,5,256]{2,0,1:T(8,128)(2,1)S(1)}, bf16[64,5,256]{2,0,1:T(8,128)(2,1)S(1)}, u32[]{:S(2)}, u32[]{:S(2)}) collective-permute-start(bf16[64,5,256]{2,0,1:T(8,128)(2,1)S(1)} %get-tuple-element.8), channel_id=1, source_target_pairs={{0,4},{4,8},{8,12},{12,16},{16,20},{20,24},{24,28},{1,5},{5,9},{9,... | collective-permute-start | bytes 491528 | tf_op jit(solution)/shard_map/ppermute | solution.py:10
  59.2 10.2 %collective-permute-start.1 = (bf16[64,5,256]{2,0,1:T(8,128)(2,1)S(1)}, bf16[64,5,256]{2,0,1:T(8,128)(2,1)}, u32[]{:S(2)}, u32[]{:S(2)}) collective-permute-start(bf16[64,5,256]{2,0,1:T(8,128)(2,1)S(1)} %get-tuple-element.9), channel_id=1, source_target_pairs={{4,0},{8,4},{12,8},{16,12},{20,16},{24,20},{28,24},{5,1},{9,5},{13... | collective-permute-start | bytes 491528 | tf_op jit(solution)/shard_map/ppermute | solution.py:10
  60.8 6.7 %copy-start.4 = (bf16[5,5,768]{2,1,0:T(8,128)(2,1)S(1)}, bf16[5,5,768]{2,1,0:T(8,128)(2,1)}, u32[]{:S(2)}) copy-start(bf16[5,5,768]{2,1,0:T(8,128)(2,1)} %param.12) | copy-start | bytes 115204
  131.5 6.6 %copy-start.1 = (bf16[64,5,768]{2,0,1:T(8,128)(2,1)}, bf16[64,5,768]{2,0,1:T(8,128)(2,1)S(1)}, u32[]{:S(2)}) copy-start(bf16[64,5,768]{2,0,1:T(8,128)(2,1)S(1)} %copy.41) | copy-start | bytes 1474564
  131.5 71.2 %copy-start.6 = (f32[256]{0:T(256)S(1)}, f32[256]{0:T(256)}, u32[]{:S(2)}) copy-start(f32[256]{0:T(256)} %param.11) | copy-start | bytes 3076
  138.1 126.0 %reduce-scatter.7.cloned.1.call-start = ((), (), s32[]{:S(2)}) async-start(), calls=%async_computation.3 | async-start | bytes 147456
Sparse Core Ops, SparseCore 0:
  138.2 62.6 reduce-scatter.4
  204.2 59.8 reduce-scatter.6
where the time goes:
time: 274 us; the launch traced here: 273 us
  waiting for transfers between devices  119 us (43%)
  local copies, waits for them, and re-layouts  67.1 us (24%)
  blocking collectives  33.1 us (12%)
  matrix products  27.9 us (10%)
  between operations  14.9 us (5%)
  other arithmetic  5.69 us (2%)
  starting transfers between devices  4.97 us (2%)
    unnamed x3, waiting for transfers between devices  61.3 us
    reduce_scatter x1, waiting for transfers between devices, shards(): shares = lax.psum_scatter(products, 'rows', scatter_dimension=0, tiled=True)  57.5 us
    all_gather x1, blocking collectives, shards(): lax.all_gather(eigvec, 'rows', axis=0, tiled=True)  27.9 us
    unnamed x24, local copies, waits for them, and re-layouts  23.4 us
    gather x2, local copies, waits for them, and re-layouts, shards(): neighbours = jnp.take(extended, neighbor, axis=2)  22.8 us
    select_n x1, local copies, waits for them, and re-layouts, shards(): neighbours = jnp.take(extended, neighbor, axis=2)  14.5 us
    dot_general x1, matrix products, shards(): jnp.einsum('bvwc,mwbc->mvc', jac_off, neighbours, preferred_element_type=...  9.62 us
    dot_general x1, matrix products, shards(): lax.dot_general(snap_rows, test_local.reshape(panel_width, var_count * ce...  6.58 us
  transfers between devices with their start and end apart: 4, of which 2 were waited for; matrix products, arithmetic and copies ran while one was open for 3% of the time, Pallas kernels for 0%

commit v1 on v0

--- a/solution.py
+++ b/solution.py
@@ -1,7 +1,37 @@
+import functools
 import jax
 import jax.numpy as jnp
 from jax import lax
 from jax.sharding import PartitionSpec as P
+
+
+def place_forms_by_axis(z_in, d_out):
+    ready = list(z_in.shape[1:])
+    ready[d_out] *= z_in.shape[0]
+    w1 = jnp.moveaxis(z_in, 0, d_out).reshape(ready)
+    return w1
+
+
+def begin_local_data(own_rows, mesh_ax):
+    total_devices = jax.lax.axis_size(mesh_ax)
+    front = own_rows[None]
+    for b in range(total_devices.bit_length() - 1):
+        x_new = 1 << b
+        state_next = jax.lax.ppermute(
+            front, mesh_ax, list(map(lambda dev_i: (dev_i, dev_i ^ x_new), range(total_devices)))
+        )
+        reply = jnp.stack([front, state_next])
+        block_last = jax.lax.axis_index(mesh_ax) >> b & 1
+        front = jnp.where(block_last == 0, reply, reply[::-1]).reshape(-1, *own_rows.shape)
+    return front
+
+
+def recast_the_edges(tile_in, sheet, array_dim):
+    piece_out = place_forms_by_axis(begin_local_data(tile_in, sheet), array_dim)
+    return piece_out
+
+
+mark_records = functools.partial(recast_the_edges, sheet="rows", array_dim=0)
 
 
 def passed_along(value, axis, steps):
@@ -22,7 +52,7 @@
     halo_slots = send_list.shape[1]
     snap_rows = snapshots.reshape(snap_count, var_count * cell_count)
     modes_sum = lax.dot_general(
-        lax.all_gather(eigvec, "rows", axis=0, tiled=True),
+        mark_records(eigvec),
         snap_rows,
         (((0,), (0,)), ((), ())),
         preferred_element_type=jnp.float32,

time: 274 us -> 260 us (0.949)
  blocking collectives: 33.1 us -> 5.25 us
  starting transfers between devices: 4.97 us -> 12.7 us
  waiting for transfers between devices: 119 us -> 122 us
    all_gather x1 -> x0, blocking collectives: 27.9 us -> none  [shards(): lax.all_gather(eigvec, 'rows', axis=0, tiled=True)]
    ppermute x0 -> x3, starting transfers between devices: none -> 7.55 us  [begin_local_data(): jax.lax.ppermute(front, mesh_ax, list(map(lambda dev_i: (dev_i, dev_i ^ x...]
    ppermute x0 -> x3, waiting for transfers between devices: none -> 2.92 us  [begin_local_data(): jax.lax.ppermute(front, mesh_ax, list(map(lambda dev_i: (dev_i, dev_i ^ x...]
    unnamed x24 -> x20, local copies, waits for them, and re-layouts: 23.4 us -> 24 us
  transfers between devices with their start and end apart: 4 -> 7, of which waited for: 2 -> 3; matrix products, arithmetic and copies ran while one was open for 3% -> 8% of each run, Pallas kernels for 0% -> 0%
where the time goes in v1:
time: 260 us; the launch traced here: 259 us
  waiting for transfers between devices  122 us (47%)
  local copies, waits for them, and re-layouts  67.9 us (26%)
  matrix products  27.9 us (11%)
  between operations  15 us (6%)
  starting transfers between devices  12.7 us (5%)
  other arithmetic  7.92 us (3%)
  blocking collectives  5.25 us (2%)
    unnamed x3, waiting for transfers between devices  61.3 us
    reduce_scatter x1, waiting for transfers between devices, shards(): shares = lax.psum_scatter(products, 'rows', scatter_dimension=0, tiled=True)  57.7 us
    unnamed x20, local copies, waits for them, and re-layouts  24 us
    gather x2, local copies, waits for them, and re-layouts, shards(): neighbours = jnp.take(extended, neighbor, axis=2)  22.8 us
    select_n x1, local copies, waits for them, and re-layouts, shards(): neighbours = jnp.take(extended, neighbor, axis=2)  14.5 us
    dot_general x1, matrix products, shards(): jnp.einsum('bvwc,mwbc->mvc', jac_off, neighbours, preferred_element_type=...  9.62 us
    ppermute x3, starting transfers between devices, begin_local_data(): jax.lax.ppermute(front, mesh_ax, list(map(lambda dev_i: (dev_i, dev_i ^ x...  7.55 us
    dot_general x1, matrix products, shards(): lax.dot_general(snap_rows, test_local.reshape(panel_width, var_count * ce...  6.59 us
  transfers between devices with their start and end apart: 7, of which 3 were waited for; matrix products, arithmetic and copies ran while one was open for 8% of the time, Pallas kernels for 0%

profile of v1, /device:TPU:0, one launch (start us, length us, event | category | flops | bytes accessed | tf_op | source)
XLA Modules:
  0.0 258.6 jit_solution(13518248508554326904)
XLA Ops:
  7.2 3.0 %collective-permute-start = (bf16[1,128,64]{1,2,0:T(8,128)(2,1)}, bf16[1,128,64]{1,2,0:T(8,128)(2,1)S(1)}, u32[]{:S(2)}, u32[]{:S(2)}) collective-permute-start(bf16[1,128,64]{1,2,0:T(8,128)(2,1)} %bitcast.73), channel_id=1, source_target_pairs={{0,4},{4,0},{8,12},{12,8},{16,20},{20,16},{24,28},{28,24},{1,5},{5... | collective-permute-start | bytes 49160 | tf_op jit(solution)/shard_map/ppermute | solution.py:20
  10.9 0.8 compare_and_fusion.1
  11.7 0.7 compare_select_fusion
  12.4 0.7 pad_maximum_fusion.3
  13.2 1.9 collective-permute-start.1
  15.7 10.6 %copy.33 = bf16[1024,5,768]{0,2,1:T(8,128)(2,1)} copy(bf16[1024,5,768]{2,0,1:T(8,128)(2,1)} %param.9) | data formatting | bytes 15728640 | tf_op args[0]
  26.4 2.7 %collective-permute-start.2 = (bf16[4,128,64]{1,2,0:T(8,128)(2,1)S(1)}, bf16[4,128,64]{1,2,0:T(8,128)(2,1)S(1)}, u32[]{:S(2)}, u32[]{:S(2)}) collective-permute-start(bf16[4,128,64]{1,2,0:T(8,128)(2,1)S(1)} %bitcast.71), channel_id=1, source_target_pairs={{0,16},{4,20},{8,24},{12,28},{16,0},{20,4},{24,8},{28,12},{1,17},{... | collective-permute-start | bytes 196616 | tf_op jit(solution)/shard_map/ppermute | solution.py:20
  29.1 2.9 %collective-permute-done.2 = bf16[4,128,64]{1,2,0:T(8,128)(2,1)S(1)} collective-permute-done((bf16[4,128,64]{1,2,0:T(8,128)(2,1)S(1)}, bf16[4,128,64]{1,2,0:T(8,128)(2,1)S(1)}, u32[]{:S(2)}, u32[]{:S(2)}) %collective-permute-start.2) | collective-permute-done | bytes 65568 | tf_op jit(solution)/shard_map/ppermute | solution.py:20
  32.2 5.7 %fusion.8 = bf16[64,5,768]{2,0,1:T(8,128)(2,1)S(1)} fusion(bf16[1024,64,1]{0,1,2:T(8,128)(2,1)S(1)} %reshape.110, bf16[1024,5,768]{0,2,1:T(8,128)(2,1)} %copy.33, pred[768]{0:T(1024)(128)(4,1)S(1)} %iota_compare_fusion), kind=kOutput, calls=%fused_computation.10 | convolution fusion | flops 503808000 | bytes 8487680 | tf_op jit(solution)/shard_map/dot_general | solution.py:54
  37.9 1.1 copy.34
  39.1 1.8 gather_fusion
  41.4 3.6 %collective-permute-start.3 = (bf16[64,5,256]{2,0,1:T(8,128)(2,1)S(1)}, bf16[64,5,256]{2,0,1:T(8,128)(2,1)S(1)}, u32[]{:S(2)}, u32[]{:S(2)}) collective-permute-start(bf16[64,5,256]{2,0,1:T(8,128)(2,1)S(1)} %get-tuple-element.8), channel_id=1, source_target_pairs={{0,4},{4,8},{8,12},{12,16},{16,20},{20,24},{24,28},{1,5},{5,9},{9,... | collective-permute-start | bytes 491528 | tf_op jit(solution)/shard_map/ppermute | solution.py:40
  45.1 1.5 collective-permute-start.4
  46.6 6.7 %copy.42 = bf16[6,5,5,768]{0,1,2,3:T(8,128)(2,1)} copy(bf16[6,5,5,768]{3,0,2,1:T(8,128)(2,1)} %param.13) | data formatting | bytes 460800 | tf_op args[4]
  53.3 1.9 copy.35
  55.2 1.0 pad_maximum_fusion
  56.2 2.9 %copy.39 = bf16[64,5,1280]{0,1,2:T(8,128)(2,1)S(1)} copy(bf16[64,5,1280]{2,0,1:T(8,128)(2,1)S(1)} %pad_maximum_fusion) | data formatting | bytes 1638400 | tf_op jit(solution)/shard_map/concatenate | solution.py:73
  59.1 12.9 %gather_fusion.1 = bf16[4608,64,5]{1,2,0:T(8,128)(2,1)} fusion(bf16[64,5,1280]{0,1,2:T(8,128)(2,1)S(1)} %copy.39, s32[5120]{0:T(1024)S(1)} %pad_clamp_fusion), kind=kCustom, calls=%fused_computation.1 | custom fusion | bytes 5916672 | tf_op jit(solution)/shard_map/jit(_take)/gather | solution.py:75
  72.0 9.9 %copy.49 = bf16[6,768,64,5]{1,0,2,3:T(8,128)(2,1)} copy(bf16[6,768,64,5]{2,3,1,0:T(8,128)(2,1)} %bitcast.69) | data formatting | bytes 5898240 | tf_op jit(solution)/shard_map/jit(_take)/gather | solution.py:75
  81.9 4.5 %select_bitcast_fusion = bf16[64,5,6,768]{3,2,0,1:T(8,128)(2,1)} fusion(bf16[6,768,64,5]{1,0,2,3:T(8,128)(2,1)} %copy.49, pred[6,768]{1,0:T(8,128)(4,1)S(1)} %compare_and_fusion), kind=kLoop, calls=%fused_computation.4 | loop fusion | flops 1474560 | bytes 5902848 | tf_op jit(solution)/shard_map/jit(_take)/select_n | solution.py:75
  86.3 14.5 %copy.41 = bf16[64,5,6,768]{0,2,1,3:T(8,128)(2,1)} copy(bf16[64,5,6,768]{3,2,0,1:T(8,128)(2,1)} %select_bitcast_fusion) | data formatting | bytes 5898240 | tf_op jit(solution)/shard_map/jit(_take)/select_n | solution.py:75
  100.9 9.6 %fusion.13 = f32[768,64,5,1]{1,2,3,0:T(8,128)S(1)} fusion(bf16[64,5,6,768]{0,2,1,3:T(8,128)(2,1)} %copy.41, bf16[6,5,5,768]{0,1,2,3:T(8,128)(2,1)} %copy.42), kind=kOutput, calls=%fused_computation.35 | convolution fusion | flops 14745600 | bytes 4162560 | tf_op jit(solution)/shard_map/bvwc,mwbc->mvc/dot_general | solution.py:76
  110.5 5.0 %fusion.4 = bf16[64,5,768]{0,1,2:T(8,128)(2,1)} fusion(f32[768,64,5,1]{1,2,3,0:T(8,128)S(1)} %fusion.13, bf16[64,5,768]{0,1,2:T(8,128)(2,1)} %copy-done, bf16[5,5,768]{1,0,2:T(8,128)(2,1)} %copy.35, pred[768]{0:T(1024)(128)(4,1)S(1)} %iota_compare_fusion), kind=kOutput, calls=%fused_computation.8 | convolution fusion | flops 3194880 | bytes 2005248 | tf_op jit(solution)/shard_map/vwc,mwc->mvc/dot_general | solution.py:74
  115.5 1.8 copy.44
  117.4 6.6 %convolution_bitcast_fusion = f32[1024,64]{0,1:T(8,128)} fusion(bf16[64,5,768]{2,0,1:T(8,128)(2,1)S(1)} %copy.44, bf16[1024,5,768]{2,0,1:T(8,128)(2,1)} %param.9), kind=kOutput, calls=%fused_computation.11 | convolution fusion | flops 503316480 | bytes 8617984 | tf_op jit(solution)/shard_map/dot_general | solution.py:80
  124.0 5.2 %all_gather.3 = bf16[128,256]{0,1:T(8,128)(2,1)S(1)} all-gather(bf16[128,64]{0,1:T(8,128)(2,1)S(1)} %copy-done.3), channel_id=1, replica_groups=mesh['rows'=8,'modes'=4] {'modes'}, dimensions={1}, use_global_device_ids=true | all-gather | bytes 81920 | tf_op jit(solution)/shard_map/all_gather | solution.py:87
  129.3 57.7 %reduce-scatter.5.cloned.1.call-done = f32[128,64]{0,1:T(8,128)} async-done(((f32[1024,64]{0,1:T(8,128)}), f32[128,64]{0,1:T(8,128)}) %reduce-scatter.5.cloned.1.call-update) | async-done | bytes 32784 | tf_op jit(solution)/shard_map/reduce_scatter | solution.py:86
  187.0 1.0 convolution_bitcast_fusion.1
  187.9 0.8 copy.50
  188.9 61.3 %reduce-scatter.7.cloned.1.call-done = f32[32,64]{1,0:T(8,128)} async-done(((f32[256,64]{1,0:T(8,128)}), f32[32,64]{1,0:T(8,128)}) %reduce-scatter.7.cloned.1.call-update) | async-done | bytes 8208
  250.2 0.8 copy.51
  251.0 0.7 copy.45
  (41 shorter events, 1.9 us)
Async XLA Ops:
  7.2 179.8 %reduce-scatter.5.cloned.1.call-start = ((), (), s32[]{:S(2)}) async-start(), calls=%async_computation.2 | async-start | bytes 294912 | tf_op jit(solution)/shard_map/reduce_scatter | solution.py:86
  7.2 5.2 %collective-permute-start = (bf16[1,128,64]{1,2,0:T(8,128)(2,1)}, bf16[1,128,64]{1,2,0:T(8,128)(2,1)S(1)}, u32[]{:S(2)}, u32[]{:S(2)}) collective-permute-start(bf16[1,128,64]{1,2,0:T(8,128)(2,1)} %bitcast.73), channel_id=1, source_target_pairs={{0,4},{4,0},{8,12},{12,8},{16,20},{20,16},{24,28},{28,24},{1,5},{5... | collective-permute-start | bytes 49160 | tf_op jit(solution)/shard_map/ppermute | solution.py:20
  13.2 13.2 %collective-permute-start.1 = (bf16[2,128,64]{1,2,0:T(8,128)(2,1)S(1)}, bf16[2,128,64]{1,2,0:T(8,128)(2,1)S(1)}, u32[]{:S(2)}, u32[]{:S(2)}) collective-permute-start(bf16[2,128,64]{1,2,0:T(8,128)(2,1)S(1)} %get-tuple-element.11), channel_id=1, source_target_pairs={{0,8},{4,12},{8,0},{12,4},{16,24},{20,28},{24,16},{28,20},{1,9},{5... | collective-permute-start | bytes 98312 | tf_op jit(solution)/shard_map/ppermute | solution.py:20
  26.4 5.6 %collective-permute-start.2 = (bf16[4,128,64]{1,2,0:T(8,128)(2,1)S(1)}, bf16[4,128,64]{1,2,0:T(8,128)(2,1)S(1)}, u32[]{:S(2)}, u32[]{:S(2)}) collective-permute-start(bf16[4,128,64]{1,2,0:T(8,128)(2,1)S(1)} %bitcast.71), channel_id=1, source_target_pairs={{0,16},{4,20},{8,24},{12,28},{16,0},{20,4},{24,8},{28,12},{1,17},{... | collective-permute-start | bytes 196616 | tf_op jit(solution)/shard_map/ppermute | solution.py:20
  37.9 8.6 %copy-start.2 = (s32[6,768]{1,0:T(8,128)S(1)}, s32[6,768]{1,0:T(8,128)}, u32[]{:S(2)}) copy-start(s32[6,768]{1,0:T(8,128)} %param.14) | copy-start | bytes 55300
  39.0 14.3 %copy-start = (bf16[64,5,768]{0,1,2:T(8,128)(2,1)}, bf16[64,5,768]{0,1,2:T(8,128)(2,1)S(1)}, u32[]{:S(2)}) copy-start(bf16[64,5,768]{0,1,2:T(8,128)(2,1)S(1)} %copy.34) | copy-start | bytes 1474564
  41.4 13.8 %collective-permute-start.3 = (bf16[64,5,256]{2,0,1:T(8,128)(2,1)S(1)}, bf16[64,5,256]{2,0,1:T(8,128)(2,1)S(1)}, u32[]{:S(2)}, u32[]{:S(2)}) collective-permute-start(bf16[64,5,256]{2,0,1:T(8,128)(2,1)S(1)} %get-tuple-element.8), channel_id=1, source_target_pairs={{0,4},{4,8},{8,12},{12,16},{16,20},{20,24},{24,28},{1,5},{5,9},{9,... | collective-permute-start | bytes 491528 | tf_op jit(solution)/shard_map/ppermute | solution.py:40
  45.1 10.1 %collective-permute-start.4 = (bf16[64,5,256]{2,0,1:T(8,128)(2,1)S(1)}, bf16[64,5,256]{2,0,1:T(8,128)(2,1)}, u32[]{:S(2)}, u32[]{:S(2)}) collective-permute-start(bf16[64,5,256]{2,0,1:T(8,128)(2,1)S(1)} %get-tuple-element.9), channel_id=1, source_target_pairs={{4,0},{8,4},{12,8},{16,12},{20,16},{24,20},{28,24},{5,1},{9,5},{13... | collective-permute-start | bytes 491528 | tf_op jit(solution)/shard_map/ppermute | solution.py:40
  46.6 6.7 %copy-start.4 = (bf16[5,5,768]{2,1,0:T(8,128)(2,1)S(1)}, bf16[5,5,768]{2,1,0:T(8,128)(2,1)}, u32[]{:S(2)}) copy-start(bf16[5,5,768]{2,1,0:T(8,128)(2,1)} %param.12) | copy-start | bytes 115204
  117.3 6.6 %copy-start.1 = (bf16[64,5,768]{2,0,1:T(8,128)(2,1)}, bf16[64,5,768]{2,0,1:T(8,128)(2,1)S(1)}, u32[]{:S(2)}) copy-start(bf16[64,5,768]{2,0,1:T(8,128)(2,1)S(1)} %copy.44) | copy-start | bytes 1474564
  117.3 6.7 %copy-start.3 = (bf16[128,64]{0,1:T(8,128)(2,1)S(1)}, bf16[128,64]{0,1:T(8,128)(2,1)}, u32[]{:S(2)}) copy-start(bf16[128,64]{0,1:T(8,128)(2,1)} %param.10) | copy-start | bytes 49156
  117.4 71.4 %copy-start.5 = (f32[256]{0:T(256)S(1)}, f32[256]{0:T(256)}, u32[]{:S(2)}) copy-start(f32[256]{0:T(256)} %param.11) | copy-start | bytes 3076
  124.0 126.2 %reduce-scatter.7.cloned.1.call-start = ((), (), s32[]{:S(2)}) async-start(), calls=%async_computation.3 | async-start | bytes 147456
Sparse Core Ops, SparseCore 0:
  124.1 62.8 reduce-scatter.4
  190.3 59.8 reduce-scatter.6
